TPU v7x, 32 devices: a whole 2x2x4 slice. The times are simulated.
32 devices in a mesh: dp: 8 (over y, x, core), block: 4 (over z).
Axes of the slice: x: 2, y: 2, z: 4, core: 2. Of those that a mesh axis runs over, the one named last changes fastest.
Arguments:
- tokens: bfloat16 [2304, 6144], P('dp', 'block'), may hold values from -6 to 6
- up_first: bfloat16 [96, 64, 256], P('block'), may hold values from -0.75 to 0.75
- up_mix: bfloat16 [256, 96, 96], replicated, may hold values from -0.625 to 0.625
- down_mix: bfloat16 [256, 96, 96], replicated, may hold values from -0.625 to 0.625
- down_last: bfloat16 [96, 64, 256], P('block'), may hold values from -0.375 to 0.375
- cotangent: bfloat16 [2304, 6144], P('dp', 'block'), may hold values from -6 to 6
Outputs:
- encoded: bfloat16 [2304, 6144], P('dp', 'block')
- grad_tokens: bfloat16 [2304, 6144], P('dp', 'block')
- grad_up_first: float32 [96, 64, 256], P('block')
- grad_down_last: float32 [96, 64, 256], P('block')
All inputs are finite; a program needn't handle non-finite values.
Results may differ from a plain program's by a relative error of at most 0.014.
Values may be sent and summed in bfloat16 or wider, within the bound.
A program may use at most 128 MiB of HBM per device.

v0:
```python
import jax
import jax.numpy as jnp
from jax import lax
from jax.sharding import PartitionSpec as P

gelu_coef = 0.7978845608028654
cubic_coef = 0.044715


def gelu_pair(values):
    inner = gelu_coef * (values + cubic_coef * values * values * values)
    tangent = jnp.tanh(inner)
    result = 0.5 * values * (1.0 + tangent)
    slope = 0.5 * (1.0 + tangent) + 0.5 * values * (1.0 - tangent * tangent) * gelu_coef * (
        1.0 + 3.0 * cubic_coef * values * values
    )
    return (result, slope)


def to_tokens(panel):
    return lax.all_to_all(panel, "block", split_axis=0, concat_axis=1, tiled=True)


def to_blocks(panel):
    return lax.all_to_all(panel, "block", split_axis=1, concat_axis=0, tiled=True)


def shards(tokens, up_first, up_mix, down_mix, down_last, cotangent):
    flt = jnp.float32
    half = jnp.bfloat16
    row_count = tokens.shape[0]
    local_blocks = up_first.shape[0]
    width_in = up_first.shape[1]
    inputs = tokens.reshape(row_count, local_blocks, width_in)
    outgrads = cotangent.reshape(row_count, local_blocks, width_in)
    first = jnp.einsum("trk,rkc->trc", inputs, up_first, preferred_element_type=flt).astype(half)
    grad_mixed = jnp.einsum("tqk,qkc->tqc", outgrads, down_last, preferred_element_type=flt).astype(
        half
    )
    first_tok = to_tokens(first)
    pre_tok = jnp.einsum("trc,csr->tsc", first_tok, up_mix, preferred_element_type=flt).astype(half)
    hidden_f, slope = gelu_pair(pre_tok.astype(flt))
    hidden_tok = hidden_f.astype(half)
    mixed_tok = jnp.einsum("tsc,cqs->tqc", hidden_tok, down_mix, preferred_element_type=flt).astype(
        half
    )
    mixed = to_blocks(mixed_tok)
    encoded = jnp.einsum("tqc,qkc->tqk", mixed, down_last, preferred_element_type=flt).astype(half)
    grad_last = jnp.einsum("tqk,tqc->qkc", outgrads, mixed, preferred_element_type=flt)
    grad_mixed_tok = to_tokens(grad_mixed)
    grad_hidden_tok = jnp.einsum(
        "tqc,cqs->tsc", grad_mixed_tok, down_mix, preferred_element_type=flt
    ).astype(half)
    grad_pre_tok = (grad_hidden_tok.astype(flt) * slope).astype(half)
    grad_first_tok = jnp.einsum(
        "tsc,csr->trc", grad_pre_tok, up_mix, preferred_element_type=flt
    ).astype(half)
    grad_first = to_blocks(grad_first_tok)
    grad_in = jnp.einsum("trc,rkc->trk", grad_first, up_first, preferred_element_type=flt).astype(
        half
    )
    grad_firstw = jnp.einsum("trk,trc->rkc", inputs, grad_first, preferred_element_type=flt)
    summed_first, summed_last = lax.psum((grad_firstw, grad_last), "dp")
    return (
        encoded.reshape(row_count, local_blocks * width_in),
        grad_in.reshape(row_count, local_blocks * width_in),
        summed_first,
        summed_last,
    )


def solution(mesh):
    placed = (
        P("dp", "block"),
        P("block", None, None),
        P(),
        P(),
        P("block", None, None),
        P("dp", "block"),
    )
    return jax.shard_map(
        shards,
        mesh=mesh,
        in_specs=placed,
        out_specs=(
            P("dp", "block"),
            P("dp", "block"),
            P("block", None, None),
            P("block", None, None),
        ),
        check_vma=False,
    )
```

profile of v0, /device:TPU:0, one launch (start us, length us, event | category | flops | bytes accessed | tf_op | source)
XLA Modules:
  0.0 484.4 jit_solution(3152034513963127786)
XLA Ops:
  7.2 0.0 copy-start
  7.2 1.7 copy.63
  8.9 0.0 copy-done
  8.9 1.1 convert_bitcast_fusion.2
  10.1 3.8 copy.64
  13.9 6.3 %all-to-all-start.2 = ((bf16[288,24,256]{2,1,0:T(8,128)(2,1)}), bf16[288,24,256]{2,1,0:T(8,128)(2,1)}, u32[]{:S(2)}, u32[]{:S(2)}) async-start(bf16[288,24,256]{2,1,0:T(8,128)(2,1)} %copy.64), calls=%async_computation.2 | async-start | bytes 7077888 | tf_op jit(solution)/shard_map/all_to_all | solution.py:21
  20.2 1.6 copy.54
  21.9 2.3 convert_bitcast_fusion.3
  24.1 3.8 copy.55
  27.9 71.5 %all-to-all-done.2 = bf16[288,24,256]{2,1,0:T(8,128)(2,1)} async-done(((bf16[288,24,256]{2,1,0:T(8,128)(2,1)}), bf16[288,24,256]{2,1,0:T(8,128)(2,1)}, u32[]{:S(2)}, u32[]{:S(2)}) %all-to-all-start.2) | async-done | bytes 3538976 | tf_op jit(solution)/shard_map/all_to_all | solution.py:21
  99.5 4.9 %all-to-all-start = ((bf16[288,24,256]{2,1,0:T(8,128)(2,1)}), bf16[288,24,256]{2,1,0:T(8,128)(2,1)}, u32[]{:S(2)}, u32[]{:S(2)}) async-start(bf16[288,24,256]{2,1,0:T(8,128)(2,1)} %copy.55), calls=%async_computation | async-start | bytes 7077888 | tf_op jit(solution)/shard_map/all_to_all | solution.py:21
  104.4 8.5 %copy.58 = bf16[256,96,96]{2,1,0:T(8,128)(2,1)} copy(bf16[256,96,96]{0,2,1:T(8,128)(2,1)} %param.8) | data formatting | bytes 9437184 | tf_op args[2]
  112.8 8.4 %copy.59 = bf16[256,96,96]{2,1,0:T(8,128)(2,1)} copy(bf16[256,96,96]{0,2,1:T(8,128)(2,1)} %param.9) | data formatting | bytes 9437184 | tf_op args[3]
  121.2 4.4 copy.65
  125.6 6.7 %copy.66 = bf16[72,96,256]{1,0,2:T(8,128)(2,1)} copy(bf16[72,96,256]{2,1,0:T(8,128)(2,1)} %bitcast.87) | data formatting | bytes 7077888 | tf_op jit(solution)/shard_map/all_to_all | solution.py:21
  132.3 50.5 %all-to-all-done = bf16[288,24,256]{2,1,0:T(8,128)(2,1)} async-done(((bf16[288,24,256]{2,1,0:T(8,128)(2,1)}), bf16[288,24,256]{2,1,0:T(8,128)(2,1)}, u32[]{:S(2)}, u32[]{:S(2)}) %all-to-all-start) | async-done | bytes 3538976 | tf_op jit(solution)/shard_map/all_to_all | solution.py:21
  182.8 4.4 copy.56
  187.1 6.6 %copy.57 = bf16[72,96,256]{1,0,2:T(8,128)(2,1)} copy(bf16[72,96,256]{2,1,0:T(8,128)(2,1)} %bitcast.88) | data formatting | bytes 7077888 | tf_op jit(solution)/shard_map/all_to_all | solution.py:21
  193.7 10.8 %convolution_convert_fusion = bf16[256,72,96]{2,1,0:T(8,128)(2,1)} fusion(bf16[72,96,256]{1,0,2:T(8,128)(2,1)} %copy.57, bf16[256,96,96]{2,1,0:T(8,128)(2,1)} %copy.58), kind=kOutput, calls=%fused_computation.25 | convolution fusion | flops 341508096 | bytes 11796480 | tf_op jit(solution)/shard_map/trc,csr->tsc/dot_general | solution.py:41
  204.5 16.1 %convert_bitcast_fusion = bf16[72,96,256]{1,0,2:T(8,128)(2,1)} fusion(bf16[256,96,96]{2,1,0:T(8,128)(2,1)} %copy.58, bf16[256,72,96]{2,1,0:T(8,128)(2,1)} %convolution_convert_fusion, bf16[72,96,256]{1,0,2:T(8,128)(2,1)} %copy.66, bf16[256,96,96]{2,1,0:T(8,128)(2,1)} %copy.59), kind=kOutput, calls=%fused_computation.15 | convolution fusion | flops 720175104 | bytes 20054016 | tf_op jit(solution)/shard_map/tsc,csr->trc/dot_general | solution.py:55
  220.6 7.3 %copy.69 = bf16[72,96,256]{2,0,1:T(8,128)(2,1)} copy(bf16[72,96,256]{1,0,2:T(8,128)(2,1)} %convert_bitcast_fusion) | data formatting | bytes 7077888 | tf_op jit(solution)/shard_map/convert_element_type | solution.py:57
  227.9 4.9 %all-to-all-start.3 = ((bf16[72,96,256]{2,0,1:T(8,128)(2,1)}), bf16[72,96,256]{2,0,1:T(8,128)(2,1)}, u32[]{:S(2)}, u32[]{:S(2)}) async-start(bf16[72,96,256]{2,0,1:T(8,128)(2,1)} %copy.69), calls=%async_computation.3 | async-start | bytes 7077888 | tf_op jit(solution)/shard_map/all_to_all | solution.py:25
  232.8 10.1 %convert_bitcast_fusion.1 = bf16[72,96,256]{1,0,2:T(8,128)(2,1)} fusion(bf16[256,96,96]{2,1,0:T(8,128)(2,1)} %copy.59, bf16[256,72,96]{2,1,0:T(8,128)(2,1)} %convolution_convert_fusion), kind=kOutput, calls=%fused_computation.16 | convolution fusion | flops 359202816 | bytes 11796480 | tf_op jit(solution)/shard_map/tsc,cqs->tqc/dot_general | solution.py:44
  242.9 7.3 %copy.60 = bf16[72,96,256]{2,0,1:T(8,128)(2,1)} copy(bf16[72,96,256]{1,0,2:T(8,128)(2,1)} %convert_bitcast_fusion.1) | data formatting | bytes 7077888 | tf_op jit(solution)/shard_map/convert_element_type | solution.py:44
  250.2 61.1 %all-to-all-done.3 = bf16[72,96,256]{2,0,1:T(8,128)(2,1)} async-done(((bf16[72,96,256]{2,0,1:T(8,128)(2,1)}), bf16[72,96,256]{2,0,1:T(8,128)(2,1)}, u32[]{:S(2)}, u32[]{:S(2)}) %all-to-all-start.3) | async-done | bytes 3538976 | tf_op jit(solution)/shard_map/all_to_all | solution.py:25
  311.2 4.7 all-to-all-start.1
  316.0 0.0 all-reduce.3.cloned.1.call-start
  316.0 4.2 copy.71
  320.2 74.4 %all-to-all-done.1 = bf16[72,96,256]{2,0,1:T(8,128)(2,1)} async-done(((bf16[72,96,256]{2,0,1:T(8,128)(2,1)}), bf16[72,96,256]{2,0,1:T(8,128)(2,1)}, u32[]{:S(2)}, u32[]{:S(2)}) %all-to-all-start.1) | async-done | bytes 3538976 | tf_op jit(solution)/shard_map/all_to_all | solution.py:25
  394.6 2.4 copy.62
  397.0 0.0 copy-start.2
  397.0 0.0 copy-start.1
  397.0 1.8 copy-done.2
  398.8 2.1 convolution_bitcast_fusion
  400.9 0.0 copy-done.1
  400.9 2.1 convolution_bitcast_fusion.1
  403.0 0.0 copy-start.3
  403.0 0.0 all-reduce.3.cloned.1.call-update
  403.1 3.3 convolution_convert_fusion.2
  406.3 1.3 copy.72
  407.7 0.0 copy-done.3
  407.7 3.3 convolution_convert_fusion.1
  411.0 1.3 copy.73
  412.3 59.8 %all-reduce.3.cloned.1.call-done = (f32[24,64,256]{2,1,0:T(8,128)}, f32[24,64,256]{2,1,0:T(8,128)}) async-done(((f32[24,64,256]{2,1,0:T(8,128)}, f32[24,64,256]{2,1,0:T(8,128)}), (f32[24,64,256]{2,1,0:T(8,128)}, f32[24,64,256]{2,1,0:T(8,128)})) %all-reduce.3.cloned.1.call-update) | async-done | bytes 3145744 | tf_op jit(solution)/shard_map/psum | solution.py:63
  472.1 2.7 copy.78
  474.8 2.7 copy.79
Async XLA Ops:
  7.2 1.7 copy-start
  13.9 85.6 %all-to-all-start.2 = ((bf16[288,24,256]{2,1,0:T(8,128)(2,1)}), bf16[288,24,256]{2,1,0:T(8,128)(2,1)}, u32[]{:S(2)}, u32[]{:S(2)}) async-start(bf16[288,24,256]{2,1,0:T(8,128)(2,1)} %copy.64), calls=%async_computation.2 | async-start | bytes 7077888 | tf_op jit(solution)/shard_map/all_to_all | solution.py:21
  99.5 83.3 %all-to-all-start = ((bf16[288,24,256]{2,1,0:T(8,128)(2,1)}), bf16[288,24,256]{2,1,0:T(8,128)(2,1)}, u32[]{:S(2)}, u32[]{:S(2)}) async-start(bf16[288,24,256]{2,1,0:T(8,128)(2,1)} %copy.55), calls=%async_computation | async-start | bytes 7077888 | tf_op jit(solution)/shard_map/all_to_all | solution.py:21
  227.9 83.4 %all-to-all-start.3 = ((bf16[72,96,256]{2,0,1:T(8,128)(2,1)}), bf16[72,96,256]{2,0,1:T(8,128)(2,1)}, u32[]{:S(2)}, u32[]{:S(2)}) async-start(bf16[72,96,256]{2,0,1:T(8,128)(2,1)} %copy.69), calls=%async_computation.3 | async-start | bytes 7077888 | tf_op jit(solution)/shard_map/all_to_all | solution.py:25
  311.2 83.4 %all-to-all-start.1 = ((bf16[72,96,256]{2,0,1:T(8,128)(2,1)}), bf16[72,96,256]{2,0,1:T(8,128)(2,1)}, u32[]{:S(2)}, u32[]{:S(2)}) async-start(bf16[72,96,256]{2,0,1:T(8,128)(2,1)} %copy.60), calls=%async_computation.1 | async-start | bytes 7077888 | tf_op jit(solution)/shard_map/all_to_all | solution.py:25
  316.0 156.2 %all-reduce.3.cloned.1.call-start = ((), (), s32[]{:S(2)}) async-start(), calls=%async_computation.4 | async-start | bytes 6291456 | tf_op jit(solution)/shard_map/psum | solution.py:63
  397.0 1.8 copy-start.2
  397.0 3.9 copy-start.1
  403.0 4.6 copy-start.3
Sparse Core Ops, SparseCore 0:
  403.2 68.9 all-reduce.2
where the time goes:
time: 486 us; the launch traced here: 484 us
  waiting for transfers between devices  317 us (65%)
  local copies, waits for them, and re-layouts  80.9 us (17%)
  matrix products  51.2 us (11%)
  starting transfers between devices  20.9 us (4%)
  between operations  14.1 us (3%)
    all_to_all x2, waiting for transfers between devices, to_blocks(): lax.all_to_all(panel, 'block', split_axis=1, concat_axis=0, tiled=True)  136 us
    all_to_all x2, waiting for transfers between devices, to_tokens(): lax.all_to_all(panel, 'block', split_axis=0, concat_axis=1, tiled=True)  122 us
    psum x1, waiting for transfers between devices, shards(): summed_first, summed_last = lax.psum((grad_firstw, grad_last), 'dp')  59.8 us
    unnamed x16, local copies, waits for them, and re-layouts  30.1 us
    all_to_all x4, local copies, waits for them, and re-layouts, to_tokens(): lax.all_to_all(panel, 'block', split_axis=0, concat_axis=1, tiled=True)  22 us
    dot_general x1, matrix products, shards(): jnp.einsum('tsc,csr->trc', grad_pre_tok, up_mix, preferred_element_type=flt)  16.1 us
    all_to_all x2, starting transfers between devices, to_tokens(): lax.all_to_all(panel, 'block', split_axis=0, concat_axis=1, tiled=True)  11.2 us
    dot_general x1, matrix products, shards(): jnp.einsum('trc,csr->tsc', first_tok, up_mix, preferred_element_type=flt)  10.8 us
  transfers between devices with their start and end apart: 5, of which 5 were waited for; matrix products, arithmetic and copies ran while one was open for 14% of the time, Pallas kernels for 0%

commit v1 on v0

v1 whole, which is shorter than its diff:
```python
import jax
import jax.numpy as jnp
from jax import lax
from jax.sharding import PartitionSpec as P

gelu_coef = 0.7978845608028654
cubic_coef = 0.044715
WIRE = jnp.bfloat16


def gelu_pair(values):
    inner = gelu_coef * (values + cubic_coef * values * values * values)
    tangent = jnp.tanh(inner)
    result = 0.5 * values * (1.0 + tangent)
    slope = 0.5 * (1.0 + tangent) + 0.5 * values * (1.0 - tangent * tangent) * gelu_coef * (
        1.0 + 3.0 * cubic_coef * values * values
    )
    return (result, slope)


def gather_weights(weights, n_dp, n_block):
    two, blocks, width, hidden = weights.shape
    part = width // n_dp
    mine = lax.dynamic_slice_in_dim(weights, lax.axis_index("dp") * part, part, 2)
    full = lax.all_gather(mine, ("block", "dp"))
    full = full.reshape(n_block, n_dp, two, blocks, part, hidden)
    full = full.transpose(2, 0, 3, 1, 4, 5)
    return full.reshape(two, n_block * blocks, width, hidden)


def scatter_grad(grad, n_dp, n_block):
    blocks, width, hidden = grad.shape
    local = blocks // n_block
    part = width // n_dp
    pieces = grad.astype(WIRE).reshape(n_block, local, n_dp, part, hidden).transpose(0, 2, 1, 3, 4)
    pieces = pieces.reshape(n_block * n_dp, local, part, hidden)
    return lax.psum_scatter(pieces, ("block", "dp"), scatter_dimension=0, tiled=True)


def spread_grads(first, last):
    full = lax.all_gather(jnp.concatenate([first, last], 0), "dp")
    n_dp, two, blocks, part, hidden = full.shape
    full = full.transpose(1, 2, 0, 3, 4).reshape(two, blocks, n_dp * part, hidden)
    full = full.astype(jnp.float32)
    return full[0], full[1]


def shards(tokens, up_first, up_mix, down_mix, down_last, cotangent, n_dp, n_block):
    flt = jnp.float32
    half = jnp.bfloat16
    rows, features = tokens.shape
    width = up_first.shape[1]
    mine = rows // n_block
    blocks = up_first.shape[0] * n_block
    both = jnp.stack([tokens.reshape(n_block, mine, features), cotangent.reshape(n_block, mine, features)], 1)
    both = lax.all_to_all(both, "block", 0, 0, tiled=True)
    both = both.reshape(n_block, 2, mine, up_first.shape[0], width)
    both = both.transpose(1, 0, 3, 2, 4).reshape(2, blocks, mine, width)
    inputs, outgrads = both[0], both[1]
    weights = gather_weights(jnp.stack([up_first, down_last]), n_dp, n_block)
    first_w, last_w = weights[0], weights[1]
    first = jnp.einsum("rtk,rkc->rtc", inputs, first_w, preferred_element_type=flt).astype(half)
    grad_mixed = jnp.einsum("qtk,qkc->qtc", outgrads, last_w, preferred_element_type=flt).astype(half)
    pre = jnp.einsum("rtc,csr->tsc", first, up_mix, preferred_element_type=flt).astype(half)
    hidden_f, slope = gelu_pair(pre.astype(flt))
    hidden = hidden_f.astype(half)
    mixed = jnp.einsum("tsc,cqs->qtc", hidden, down_mix, preferred_element_type=flt).astype(half)
    grad_last = jnp.einsum("qtk,qtc->qkc", outgrads, mixed, preferred_element_type=flt)
    part_last = scatter_grad(grad_last, n_dp, n_block)
    encoded = jnp.einsum("qtc,qkc->qtk", mixed, last_w, preferred_element_type=flt).astype(half)
    grad_hidden = jnp.einsum("qtc,cqs->tsc", grad_mixed, down_mix, preferred_element_type=flt).astype(half)
    grad_pre = (grad_hidden.astype(flt) * slope).astype(half)
    grad_first = jnp.einsum("tsc,csr->rtc", grad_pre, up_mix, preferred_element_type=flt).astype(half)
    grad_firstw = jnp.einsum("rtk,rtc->rkc", inputs, grad_first, preferred_element_type=flt)
    part_first = scatter_grad(grad_firstw, n_dp, n_block)
    grad_in = jnp.einsum("rtc,rkc->rtk", grad_first, first_w, preferred_element_type=flt).astype(half)
    outs = jnp.stack([encoded, grad_in]).reshape(2, n_block, blocks // n_block, mine, width)
    outs = outs.transpose(1, 0, 3, 2, 4).reshape(n_block, 2, mine, features)
    outs = lax.all_to_all(outs, "block", 0, 0, tiled=True)
    summed_first, summed_last = spread_grads(part_first, part_last)
    return (
        outs[:, 0].reshape(rows, features),
        outs[:, 1].reshape(rows, features),
        summed_first,
        summed_last,
    )


def solution(mesh):
    n_dp, n_block = mesh.shape["dp"], mesh.shape["block"]

    def run(*args):
        return shards(*args, n_dp, n_block)

    placed = (
        P("dp", "block"),
        P("block", None, None),
        P(),
        P(),
        P("block", None, None),
        P("dp", "block"),
    )
    return jax.shard_map(
        run,
        mesh=mesh,
        in_specs=placed,
        out_specs=(
            P("dp", "block"),
            P("dp", "block"),
            P("block", None, None),
            P("block", None, None),
        ),
        check_vma=False,
    )
```

time: 486 us -> 408 us (0.84)
  waiting for transfers between devices: 317 us -> 233 us
  starting transfers between devices: 20.9 us -> 10 us
  other arithmetic: 0 us -> 10.7 us
    all_to_all x4 -> x2, waiting for transfers between devices: 258 us -> 32.3 us  [the longest x1 32.3 us: shards(): both = lax.all_to_all(both, 'block', 0, 0, tiled=True)]
    reduce_scatter x0 -> x2, waiting for transfers between devices: none -> 154 us  [scatter_grad(): lax.psum_scatter(pieces, ('block', 'dp'), scatter_dimension=0, tiled=True)]
    psum x1 -> x0, waiting for transfers between devices: 59.8 us -> none  [shards(): summed_first, summed_last = lax.psum((grad_firstw, grad_last), 'dp')]
    all_gather x0 -> x2, waiting for transfers between devices: none -> 46.9 us  [the longest x1 24 us: spread_grads(): full = lax.all_gather(jnp.concatenate([first, last], 0), 'dp')]
    all_to_all x6 -> x0, local copies, waits for them, and re-layouts: 28.5 us -> none  [the longest x4 22 us: to_tokens(): lax.all_to_all(panel, 'block', split_axis=0, concat_axis=1, tiled=True)]
    reshape x0 -> x5, local copies, waits for them, and re-layouts: none -> 15.2 us  [the longest x1 4.25 us: shards(): both = both.reshape(n_block, 2, mine, up_first.shape[0], width)]
    slice x0 -> x6, local copies, waits for them, and re-layouts: none -> 12.6 us  [the longest x3 8.78 us: shards(): inputs, outgrads = (both[0], both[1])]
    all_to_all x4 -> x2, starting transfers between devices: 20.8 us -> 9.9 us  [the longest x1 6.32 us: shards(): both = lax.all_to_all(both, 'block', 0, 0, tiled=True)]
  transfers between devices with their start and end apart: 5 -> 6, of which waited for: 5 -> 5; matrix products, arithmetic and copies ran while one was open for 14% -> 25% of each run, Pallas kernels for 0% -> 0%
where the time goes in v1:
time: 408 us; the launch traced here: 407 us
  waiting for transfers between devices  233 us (57%)
  local copies, waits for them, and re-layouts  85.1 us (21%)
  matrix products  54.2 us (13%)
  between operations  13.9 us (3%)
  other arithmetic  10.7 us (3%)
  starting transfers between devices  10 us (2%)
    reduce_scatter x2, waiting for transfers between devices, scatter_grad(): lax.psum_scatter(pieces, ('block', 'dp'), scatter_dimension=0, tiled=True)  154 us
    all_to_all x1, waiting for transfers between devices, shards(): both = lax.all_to_all(both, 'block', 0, 0, tiled=True)  32.3 us
    all_gather x1, waiting for transfers between devices, spread_grads(): full = lax.all_gather(jnp.concatenate([first, last], 0), 'dp')  24 us
    all_gather x1, waiting for transfers between devices, gather_weights(): full = lax.all_gather(mine, ('block', 'dp'))  22.8 us
    unnamed x12, local copies, waits for them, and re-layouts  20.7 us
    dot_general x1, matrix products, shards(): jnp.einsum('tsc,csr->rtc', grad_pre, up_mix, preferred_element_type=flt)  16.3 us
    slice x3, local copies, waits for them, and re-layouts, shards(): inputs, outgrads = (both[0], both[1])  8.78 us
    dot_general x1, matrix products, shards(): jnp.einsum('tsc,cqs->qtc', hidden, down_mix, preferred_element_type=flt)  8.59 us
  transfers between devices with their start and end apart: 6, of which 5 were waited for; matrix products, arithmetic and copies ran while one was open for 25% of the time, Pallas kernels for 0%

profile of v1, /device:TPU:0, one launch (start us, length us, event | category | flops | bytes accessed | tf_op | source)
XLA Modules:
  0.0 406.9 jit_solution(9393704664406195478)
XLA Ops:
  7.2 0.0 all-gather.5.cloned.1.call-start
  7.2 1.6 fusion.25
  8.9 0.0 all-gather.5.cloned.1.call-update
  8.9 2.8 pad_maximum_fusion
  11.7 6.3 %all-to-all-start = ((bf16[4,2,72,1536]{3,2,1,0:T(8,128)(2,1)}), bf16[4,2,72,1536]{3,2,1,0:T(8,128)(2,1)}, u32[]{:S(2)}, u32[]{:S(2)}) async-start(bf16[4,2,72,1536]{3,2,1,0:T(8,128)(2,1)} %pad_maximum_fusion), calls=%async_computation | async-start | bytes 3538944 | tf_op jit(solution)/shard_map/all_to_all | solution.py:56
  18.0 8.4 %copy.69 = bf16[256,96,96]{2,1,0:T(8,128)(2,1)} copy(bf16[256,96,96]{0,2,1:T(8,128)(2,1)} %param.8) | data formatting | bytes 9437184 | tf_op args[2]
  26.4 8.4 %copy.70 = bf16[256,96,96]{2,1,0:T(8,128)(2,1)} copy(bf16[256,96,96]{0,2,1:T(8,128)(2,1)} %param.9) | data formatting | bytes 9437184 | tf_op args[3]
  34.9 32.3 %all-to-all-done = bf16[4,2,72,1536]{3,2,1,0:T(8,128)(2,1)} async-done(((bf16[4,2,72,1536]{3,2,1,0:T(8,128)(2,1)}), bf16[4,2,72,1536]{3,2,1,0:T(8,128)(2,1)}, u32[]{:S(2)}, u32[]{:S(2)}) %all-to-all-start) | async-done | bytes 1769504 | tf_op jit(solution)/shard_map/all_to_all | solution.py:56
  67.1 4.2 %reshape.50 = bf16[4,2,72,24,64]{4,3,2,1,0:T(8,128)(2,1)S(1)} reshape(bf16[4,2,72,1536]{3,2,1,0:T(8,128)(2,1)} %all-to-all-done) | data formatting | bytes 3538944 | tf_op jit(solution)/shard_map/reshape | solution.py:57
  71.4 2.4 fusion.36
  73.8 4.0 copy.72
  77.7 2.4 copy.66
  80.2 22.8 %all-gather.5.cloned.1.call-done = bf16[64,24,8,256]{3,2,1,0:T(8,128)(2,1)} async-done(((bf16[2,24,8,256]{3,2,1,0:T(8,128)(2,1)}), bf16[64,24,8,256]{3,2,1,0:T(8,128)(2,1)}) %all-gather.5.cloned.1.call-update) | async-done | bytes 6291472 | tf_op jit(solution)/shard_map/all_gather | solution.py:25
  103.0 3.7 copy.88
  106.7 2.2 fusion.35
  108.9 1.7 copy-done
  110.7 1.2 convolution_convert_fusion.2
  111.8 5.3 %copy.68 = bf16[96,72,256]{0,1,2:T(8,128)(2,1)} copy(bf16[96,72,256]{2,1,0:T(8,128)(2,1)S(1)} %convolution_convert_fusion.2) | data formatting | bytes 7077888 | tf_op jit(solution)/shard_map/convert_element_type | solution.py:62
  117.1 8.6 %convolution_convert_fusion = bf16[256,72,96]{2,1,0:T(8,128)(2,1)S(1)} fusion(bf16[96,72,256]{0,1,2:T(8,128)(2,1)} %copy.68, bf16[256,96,96]{2,1,0:T(8,128)(2,1)} %copy.69), kind=kOutput, calls=%fused_computation.26 | convolution fusion | flops 341508096 | bytes 11796480 | tf_op jit(solution)/shard_map/rtc,csr->tsc/dot_general | solution.py:64
  125.7 2.1 copy-done.4
  127.8 8.6 %convert_bitcast_fusion.1 = bf16[96,72,256]{0,1,2:T(8,128)(2,1)} fusion(bf16[256,96,96]{2,1,0:T(8,128)(2,1)} %copy.70, bf16[256,72,96]{2,1,0:T(8,128)(2,1)S(1)} %convolution_convert_fusion), kind=kOutput, calls=%fused_computation.17 | convolution fusion | flops 359202816 | bytes 11796480 | tf_op jit(solution)/shard_map/tsc,cqs->qtc/dot_general | solution.py:67
  136.4 6.4 %copy.71 = bf16[96,72,256]{2,1,0:T(8,128)(2,1)S(1)} copy(bf16[96,72,256]{0,1,2:T(8,128)(2,1)} %convert_bitcast_fusion.1) | data formatting | bytes 7077888 | tf_op jit(solution)/shard_map/convert_element_type | solution.py:67
  142.8 2.4 convolution_convert_fusion.3
  145.1 2.0 copy.82
  147.2 0.0 reduce-scatter.5.cloned.1.call-update
  147.2 0.0 reduce-scatter.3.cloned.1.call-start
  147.2 5.4 %convolution_convert_fusion.1 = bf16[96,72,256]{2,1,0:T(8,128)(2,1)} fusion(bf16[96,72,64]{1,2,0:T(8,128)(2,1)} %bitcast.99, bf16[96,64,256]{2,1,0:T(8,128)(2,1)} %bitcast.92), kind=kOutput, calls=%fused_computation.27 | convolution fusion | flops 228261888 | bytes 7569408 | tf_op jit(solution)/shard_map/qtk,qkc->qtc/dot_general | solution.py:63
  152.6 7.2 %copy.73 = bf16[96,72,256]{0,1,2:T(8,128)(2,1)} copy(bf16[96,72,256]{2,1,0:T(8,128)(2,1)} %convolution_convert_fusion.1) | data formatting | bytes 7077888 | tf_op jit(solution)/shard_map/convert_element_type | solution.py:63
  159.8 16.3 %convert_bitcast_fusion = bf16[96,72,256]{0,1,2:T(8,128)(2,1)} fusion(bf16[256,96,96]{2,1,0:T(8,128)(2,1)} %copy.69, bf16[256,72,96]{2,1,0:T(8,128)(2,1)} %copy-done.4, bf16[96,72,256]{0,1,2:T(8,128)(2,1)} %copy.73, bf16[256,96,96]{2,1,0:T(8,128)(2,1)} %copy.70), kind=kOutput, calls=%fused_computation.16 | convolution fusion | flops 720175104 | bytes 20054016 | tf_op jit(solution)/shard_map/tsc,csr->rtc/dot_general | solution.py:73
  176.1 7.4 %copy.76 = bf16[96,72,256]{2,1,0:T(8,128)(2,1)} copy(bf16[96,72,256]{0,1,2:T(8,128)(2,1)} %convert_bitcast_fusion) | data formatting | bytes 7077888 | tf_op jit(solution)/shard_map/convert_element_type | solution.py:73
  183.5 3.5 convolution_convert_fusion.4
  187.0 2.1 copy.80
  189.1 4.1 %convolution_convert_fusion.6 = bf16[96,72,64]{1,2,0:T(8,128)(2,1)} fusion(bf16[96,72,256]{2,1,0:T(8,128)(2,1)S(1)} %copy.71, bf16[96,64,256]{2,1,0:T(8,128)(2,1)} %bitcast.93), kind=kOutput, calls=%fused_computation.33 | convolution fusion | flops 226934784 | bytes 7569408 | tf_op jit(solution)/shard_map/qtc,qkc->qtk/dot_general | solution.py:70
  193.2 4.3 %copy.77 = bf16[1,4,24,72,64]{4,2,3,0,1:T(8,128)(2,1)} copy(bf16[1,4,24,72,64]{3,4,2,1,0:T(8,128)(2,1)} %bitcast.105) | data formatting | bytes 1769472 | tf_op jit(solution)/shard_map/stack | solution.py:77
  197.5 4.2 %convolution_convert_fusion.5 = bf16[96,72,64]{1,2,0:T(8,128)(2,1)} fusion(bf16[96,72,256]{2,1,0:T(8,128)(2,1)} %copy.76, bf16[96,64,256]{2,1,0:T(8,128)(2,1)S(1)} %bitcast.91), kind=kOutput, calls=%fused_computation.32 | convolution fusion | flops 226934784 | bytes 7569408 | tf_op jit(solution)/shard_map/rtc,rkc->rtk/dot_general | solution.py:76
  201.8 4.0 copy.78
  205.7 2.9 maximum_bitcast_fusion
  208.6 3.2 reshape.52
  211.7 3.6 all-to-all-start.1
  215.3 0.0 all-gather.7.cloned.1.call-start
  215.4 49.9 %reduce-scatter.5.cloned.1.call-done = bf16[1,24,8,256]{3,2,1,0:T(8,128)(2,1)} async-done(((bf16[32,24,8,256]{3,2,1,0:T(8,128)(2,1)}), bf16[1,24,8,256]{3,2,1,0:T(8,128)(2,1)}) %reduce-scatter.5.cloned.1.call-update) | async-done | bytes 98320 | tf_op jit(solution)/shard_map/reduce_scatter | solution.py:37
  265.3 103.9 %reduce-scatter.3.cloned.1.call-done = bf16[1,24,8,256]{3,2,1,0:T(8,128)(2,1)} async-done(((bf16[32,24,8,256]{3,2,1,0:T(8,128)(2,1)}), bf16[1,24,8,256]{3,2,1,0:T(8,128)(2,1)}) %reduce-scatter.3.cloned.1.call-update) | async-done | bytes 98320 | tf_op jit(solution)/shard_map/reduce_scatter | solution.py:37
  369.2 1.6 pad_maximum_fusion.1
  370.9 1.3 fusion.38
  372.2 24.0 %all-gather.7.cloned.1.call-done = bf16[16,24,8,256]{3,2,1,0:T(8,128)(2,1)} async-done(((bf16[2,24,8,256]{3,2,1,0:T(8,128)(2,1)}), bf16[16,24,8,256]{3,2,1,0:T(8,128)(2,1)}) %all-gather.7.cloned.1.call-update) | async-done | bytes 1572880 | tf_op jit(solution)/shard_map/all_gather | solution.py:41
  396.2 1.7 convert_bitcast_fusion.2
  398.0 0.3 fusion.37
  398.3 2.1 copy_bitcast_fusion.1
  (12 shorter events, 0.1 us)
Async XLA Ops:
  7.2 95.8 %all-gather.5.cloned.1.call-start = ((), (), s32[]{:S(2)}) async-start(), calls=%async_computation.6 | async-start | bytes 6488064 | tf_op jit(solution)/shard_map/all_gather | solution.py:25
  11.7 55.4 %all-to-all-start = ((bf16[4,2,72,1536]{3,2,1,0:T(8,128)(2,1)}), bf16[4,2,72,1536]{3,2,1,0:T(8,128)(2,1)}, u32[]{:S(2)}, u32[]{:S(2)}) async-start(bf16[4,2,72,1536]{3,2,1,0:T(8,128)(2,1)} %pad_maximum_fusion), calls=%async_computation | async-start | bytes 3538944 | tf_op jit(solution)/shard_map/all_to_all | solution.py:56
  18.0 247.2 %reduce-scatter.5.cloned.1.call-start = ((), (), s32[]{:S(2)}) async-start(), calls=%async_computation.5 | async-start | bytes 3244032 | tf_op jit(solution)/shard_map/reduce_scatter | solution.py:37
  73.8 4.0 copy-start.3
  106.7 4.0 copy-start.2
  108.9 1.7 copy-start
  125.7 2.1 copy-start.4
  147.2 222.0 %reduce-scatter.3.cloned.1.call-start = ((), (), s32[]{:S(2)}) async-start(), calls=%async_computation.4 | async-start | bytes 3244032 | tf_op jit(solution)/shard_map/reduce_scatter | solution.py:37
  193.2 4.3 %copy-start.1 = (bf16[1,4,24,8,8,256]{5,4,3,2,1,0:T(8,128)(2,1)S(1)}, bf16[1,4,24,8,8,256]{5,4,3,2,1,0:T(8,128)(2,1)}, u32[]{:S(2)}) copy-start(bf16[1,4,24,8,8,256]{5,4,3,2,1,0:T(8,128)(2,1)} %copy-done) | copy-start | bytes 9437188
  211.7 159.1 %all-to-all-start.1 = ((bf16[4,2,72,1536]{3,2,1,0:T(8,128)(2,1)}), bf16[4,2,72,1536]{3,2,1,0:T(8,128)(2,1)S(1)}, u32[]{:S(2)}, u32[]{:S(2)}) async-start(bf16[4,2,72,1536]{3,2,1,0:T(8,128)(2,1)} %reshape.52), calls=%async_computation.1 | async-start | bytes 3538944 | tf_op jit(solution)/shard_map/all_to_all | solution.py:79
  215.3 180.9 %all-gather.7.cloned.1.call-start = ((), (), s32[]{:S(2)}) async-start(), calls=%async_computation.7 | async-start | bytes 1769472 | tf_op jit(solution)/shard_map/all_gather | solution.py:41
Sparse Core Ops, SparseCore 0:
  11.4 91.5 all-gather.4
  147.3 117.8 reduce-scatter.4
  270.7 98.4 reduce-scatter.2
  371.5 24.6 all-gather.6

commit v2 on v1

--- a/solution.py
+++ b/solution.py
@@ -5,7 +5,6 @@
 
 gelu_coef = 0.7978845608028654
 cubic_coef = 0.044715
-WIRE = jnp.bfloat16
 
 
 def gelu_pair(values):
@@ -28,21 +27,8 @@
     return full.reshape(two, n_block * blocks, width, hidden)
 
 
-def scatter_grad(grad, n_dp, n_block):
-    blocks, width, hidden = grad.shape
-    local = blocks // n_block
-    part = width // n_dp
-    pieces = grad.astype(WIRE).reshape(n_block, local, n_dp, part, hidden).transpose(0, 2, 1, 3, 4)
-    pieces = pieces.reshape(n_block * n_dp, local, part, hidden)
-    return lax.psum_scatter(pieces, ("block", "dp"), scatter_dimension=0, tiled=True)
-
-
-def spread_grads(first, last):
-    full = lax.all_gather(jnp.concatenate([first, last], 0), "dp")
-    n_dp, two, blocks, part, hidden = full.shape
-    full = full.transpose(1, 2, 0, 3, 4).reshape(two, blocks, n_dp * part, hidden)
-    full = full.astype(jnp.float32)
-    return full[0], full[1]
+def to_blocks(panel):
+    return lax.all_to_all(panel, "block", split_axis=1, concat_axis=0, tiled=True)
 
 
 def shards(tokens, up_first, up_mix, down_mix, down_last, cotangent, n_dp, n_block):
@@ -64,23 +50,23 @@
     pre = jnp.einsum("rtc,csr->tsc", first, up_mix, preferred_element_type=flt).astype(half)
     hidden_f, slope = gelu_pair(pre.astype(flt))
     hidden = hidden_f.astype(half)
-    mixed = jnp.einsum("tsc,cqs->qtc", hidden, down_mix, preferred_element_type=flt).astype(half)
-    grad_last = jnp.einsum("qtk,qtc->qkc", outgrads, mixed, preferred_element_type=flt)
-    part_last = scatter_grad(grad_last, n_dp, n_block)
-    encoded = jnp.einsum("qtc,qkc->qtk", mixed, last_w, preferred_element_type=flt).astype(half)
+    mixed_tok = jnp.einsum("tsc,cqs->tqc", hidden, down_mix, preferred_element_type=flt).astype(half)
+    mixed = to_blocks(mixed_tok)
     grad_hidden = jnp.einsum("qtc,cqs->tsc", grad_mixed, down_mix, preferred_element_type=flt).astype(half)
     grad_pre = (grad_hidden.astype(flt) * slope).astype(half)
-    grad_first = jnp.einsum("tsc,csr->rtc", grad_pre, up_mix, preferred_element_type=flt).astype(half)
-    grad_firstw = jnp.einsum("rtk,rtc->rkc", inputs, grad_first, preferred_element_type=flt)
-    part_first = scatter_grad(grad_firstw, n_dp, n_block)
-    grad_in = jnp.einsum("rtc,rkc->rtk", grad_first, first_w, preferred_element_type=flt).astype(half)
-    outs = jnp.stack([encoded, grad_in]).reshape(2, n_block, blocks // n_block, mine, width)
-    outs = outs.transpose(1, 0, 3, 2, 4).reshape(n_block, 2, mine, features)
-    outs = lax.all_to_all(outs, "block", 0, 0, tiled=True)
-    summed_first, summed_last = spread_grads(part_first, part_last)
+    grad_first_tok = jnp.einsum("tsc,csr->trc", grad_pre, up_mix, preferred_element_type=flt).astype(half)
+    own_in = tokens.reshape(rows, up_first.shape[0], width)
+    own_out = cotangent.reshape(rows, up_first.shape[0], width)
+    grad_last = jnp.einsum("tqk,tqc->qkc", own_out, mixed, preferred_element_type=flt)
+    summed_last = lax.psum(grad_last, "dp")
+    grad_first = to_blocks(grad_first_tok)
+    encoded = jnp.einsum("tqc,qkc->tqk", mixed, down_last, preferred_element_type=flt).astype(half)
+    grad_firstw = jnp.einsum("trk,trc->rkc", own_in, grad_first, preferred_element_type=flt)
+    summed_first = lax.psum(grad_firstw, "dp")
+    grad_in = jnp.einsum("trc,rkc->trk", grad_first, up_first, preferred_element_type=flt).astype(half)
     return (
-        outs[:, 0].reshape(rows, features),
-        outs[:, 1].reshape(rows, features),
+        encoded.reshape(rows, features),
+        grad_in.reshape(rows, features),
         summed_first,
         summed_last,
     )

time: 408 us -> 415 us (1.017)
  waiting for transfers between devices: 233 us -> 245 us
  other arithmetic: 10.7 us -> 4.47 us
  starting transfers between devices: 10 us -> 14.9 us
    reduce_scatter x2 -> x0, waiting for transfers between devices: 154 us -> none  [scatter_grad(): lax.psum_scatter(pieces, ('block', 'dp'), scatter_dimension=0, tiled=True)]
    all_to_all x1 -> x2, waiting for transfers between devices: 0.01 us -> 134 us  [to_blocks(): lax.all_to_all(panel, 'block', split_axis=1, concat_axis=0, tiled=True)]
    psum x0 -> x1, waiting for transfers between devices: none -> 57.5 us  [shards(): summed_first = lax.psum(grad_firstw, 'dp')]
    all_gather x1 -> x0, waiting for transfers between devices: 24 us -> none  [spread_grads(): full = lax.all_gather(jnp.concatenate([first, last], 0), 'dp')]
    unnamed x12 -> x20, local copies, waits for them, and re-layouts: 20.7 us -> 32.2 us
    reshape x4 -> x0, local copies, waits for them, and re-layouts: 10.9 us -> none  [the longest x2 4.11 us: scatter_grad(): grad.astype(WIRE).reshape(n_block, local, n_dp, part, hidden)]
    another operation x2 -> x0, local copies, waits for them, and re-layouts: 8.29 us -> none  [shards(): jnp.stack([encoded, grad_in])]
    slice x1 -> x3, local copies, waits for them, and re-layouts: 2.23 us -> 7.96 us  [shards(): first_w, last_w = (weights[0], weights[1])]
  transfers between devices with their start and end apart: 6 -> 5, of which waited for: 5 -> 5; matrix products, arithmetic and copies ran while one was open for 25% -> 17% of each run, Pallas kernels for 0% -> 0%
where the time goes in v2:
time: 415 us; the launch traced here: 413 us
  waiting for transfers between devices  245 us (59%)
  local copies, waits for them, and re-layouts  84.5 us (20%)
  matrix products  50.1 us (12%)
  starting transfers between devices  14.9 us (4%)
  between operations  14.2 us (3%)
  other arithmetic  4.47 us (1%)
    all_to_all x2, waiting for transfers between devices, to_blocks(): lax.all_to_all(panel, 'block', split_axis=1, concat_axis=0, tiled=True)  134 us
    psum x1, waiting for transfers between devices, shards(): summed_first = lax.psum(grad_firstw, 'dp')  57.5 us
    unnamed x20, local copies, waits for them, and re-layouts  32.2 us
    all_to_all x1, waiting for transfers between devices, shards(): both = lax.all_to_all(both, 'block', 0, 0, tiled=True)  32.1 us
    all_gather x1, waiting for transfers between devices, gather_weights(): full = lax.all_gather(mine, ('block', 'dp'))  21.6 us
    dot_general x1, matrix products, shards(): jnp.einsum('tsc,csr->trc', grad_pre, up_mix, preferred_element_type=flt)  16.2 us
    dot_general x1, matrix products, shards(): jnp.einsum('rtc,csr->tsc', first, up_mix, preferred_element_type=flt)  10.7 us
    dot_general x1, matrix products, shards(): jnp.einsum('tsc,cqs->tqc', hidden, down_mix, preferred_element_type=flt)  10.1 us
  transfers between devices with their start and end apart: 5, of which 5 were waited for; matrix products, arithmetic and copies ran while one was open for 17% of the time, Pallas kernels for 0%

profile of v2, /device:TPU:0, one launch (start us, length us, event | category | flops | bytes accessed | tf_op | source)
XLA Modules:
  0.0 413.4 jit_solution(11678984243374666687)
XLA Ops:
  7.2 0.0 all-gather.3.cloned.1.call-start
  7.2 1.6 fusion.25
  8.9 0.0 all-gather.3.cloned.1.call-update
  8.9 2.8 pad_maximum_fusion
  11.7 6.3 %all-to-all-start = ((bf16[4,2,72,1536]{3,2,1,0:T(8,128)(2,1)}), bf16[4,2,72,1536]{3,2,1,0:T(8,128)(2,1)}, u32[]{:S(2)}, u32[]{:S(2)}) async-start(bf16[4,2,72,1536]{3,2,1,0:T(8,128)(2,1)} %pad_maximum_fusion), calls=%async_computation | async-start | bytes 3538944 | tf_op jit(solution)/shard_map/all_to_all | solution.py:42
  18.0 8.5 %copy.59 = bf16[256,96,96]{2,1,0:T(8,128)(2,1)} copy(bf16[256,96,96]{0,2,1:T(8,128)(2,1)} %param.8) | data formatting | bytes 9437184 | tf_op args[2]
  26.6 8.5 %copy.60 = bf16[256,96,96]{2,1,0:T(8,128)(2,1)} copy(bf16[256,96,96]{0,2,1:T(8,128)(2,1)} %param.9) | data formatting | bytes 9437184 | tf_op args[3]
  35.1 32.1 %all-to-all-done = bf16[4,2,72,1536]{3,2,1,0:T(8,128)(2,1)} async-done(((bf16[4,2,72,1536]{3,2,1,0:T(8,128)(2,1)}), bf16[4,2,72,1536]{3,2,1,0:T(8,128)(2,1)}, u32[]{:S(2)}, u32[]{:S(2)}) %all-to-all-start) | async-done | bytes 1769504 | tf_op jit(solution)/shard_map/all_to_all | solution.py:42
  67.1 4.2 %reshape.36 = bf16[4,2,72,24,64]{4,3,2,1,0:T(8,128)(2,1)S(1)} reshape(bf16[4,2,72,1536]{3,2,1,0:T(8,128)(2,1)} %all-to-all-done) | data formatting | bytes 3538944 | tf_op jit(solution)/shard_map/reshape | solution.py:43
  71.4 2.4 fusion.36
  73.8 3.8 copy.56
  77.6 3.8 copy.64
  81.4 21.6 %all-gather.3.cloned.1.call-done = bf16[64,24,8,256]{3,2,1,0:T(8,128)(2,1)} async-done(((bf16[2,24,8,256]{3,2,1,0:T(8,128)(2,1)}), bf16[64,24,8,256]{3,2,1,0:T(8,128)(2,1)}) %all-gather.3.cloned.1.call-update) | async-done | bytes 6291472 | tf_op jit(solution)/shard_map/all_gather | solution.py:24
  103.0 5.1 %fusion.35 = (bf16[1,4,24,8,8,256]{5,4,2,0,3,1:T(8,128)(2,1)}, bf16[1,4,24,8,8,256]{5,4,2,0,3,1:T(8,128)(2,1)S(1)}) fusion(bf16[2,4,24,8,8,256]{5,4,2,0,3,1:T(8,128)(2,1)} %bitcast.97), kind=kLoop, calls=%fused_computation.43 | loop fusion | bytes 12582912 | tf_op jit(solution)/shard_map/slice | solution.py:47
  108.1 0.4 copy.57
  108.6 1.0 copy-done.3
  109.5 1.2 convolution_convert_fusion.2
  110.7 5.3 %copy.58 = bf16[96,72,256]{0,1,2:T(8,128)(2,1)} copy(bf16[96,72,256]{2,1,0:T(8,128)(2,1)S(1)} %convolution_convert_fusion.2) | data formatting | bytes 7077888 | tf_op jit(solution)/shard_map/convert_element_type | solution.py:48
  116.0 2.4 copy.65
  118.5 0.0 copy-done.2
  118.5 1.2 convolution_convert_fusion.1
  119.7 5.3 %copy.66 = bf16[96,72,256]{0,1,2:T(8,128)(2,1)} copy(bf16[96,72,256]{2,1,0:T(8,128)(2,1)S(1)} %convolution_convert_fusion.1) | data formatting | bytes 7077888 | tf_op jit(solution)/shard_map/convert_element_type | solution.py:49
  125.0 10.7 %convolution_convert_fusion = bf16[256,72,96]{2,1,0:T(8,128)(2,1)} fusion(bf16[96,72,256]{0,1,2:T(8,128)(2,1)} %copy.58, bf16[256,96,96]{2,1,0:T(8,128)(2,1)} %copy.59), kind=kOutput, calls=%fused_computation.23 | convolution fusion | flops 341508096 | bytes 11796480 | tf_op jit(solution)/shard_map/rtc,csr->tsc/dot_general | solution.py:50
  135.6 16.2 %convert_bitcast_fusion = bf16[72,96,256]{1,0,2:T(8,128)(2,1)} fusion(bf16[256,96,96]{2,1,0:T(8,128)(2,1)} %copy.59, bf16[256,72,96]{2,1,0:T(8,128)(2,1)} %convolution_convert_fusion, bf16[96,72,256]{0,1,2:T(8,128)(2,1)} %copy.66, bf16[256,96,96]{2,1,0:T(8,128)(2,1)} %copy.60), kind=kOutput, calls=%fused_computation.15 | convolution fusion | flops 720175104 | bytes 20054016 | tf_op jit(solution)/shard_map/tsc,csr->trc/dot_general | solution.py:57
  151.8 7.3 %copy.69 = bf16[72,96,256]{2,0,1:T(8,128)(2,1)} copy(bf16[72,96,256]{1,0,2:T(8,128)(2,1)} %convert_bitcast_fusion) | data formatting | bytes 7077888 | tf_op jit(solution)/shard_map/convert_element_type | solution.py:57
  159.1 3.7 all-to-all-start.2
  162.8 10.1 %convert_bitcast_fusion.1 = bf16[72,96,256]{1,0,2:T(8,128)(2,1)} fusion(bf16[256,96,96]{2,1,0:T(8,128)(2,1)} %copy.60, bf16[256,72,96]{2,1,0:T(8,128)(2,1)} %convolution_convert_fusion), kind=kOutput, calls=%fused_computation.16 | convolution fusion | flops 359202816 | bytes 11796480 | tf_op jit(solution)/shard_map/tsc,cqs->tqc/dot_general | solution.py:53
  172.9 7.3 %copy.61 = bf16[72,96,256]{2,0,1:T(8,128)(2,1)} copy(bf16[72,96,256]{1,0,2:T(8,128)(2,1)} %convert_bitcast_fusion.1) | data formatting | bytes 7077888 | tf_op jit(solution)/shard_map/convert_element_type | solution.py:53
  180.2 62.4 %all-to-all-done.2 = bf16[72,96,256]{2,0,1:T(8,128)(2,1)S(1)} async-done(((bf16[72,96,256]{2,0,1:T(8,128)(2,1)}), bf16[72,96,256]{2,0,1:T(8,128)(2,1)S(1)}, u32[]{:S(2)}, u32[]{:S(2)}) %all-to-all-start.2) | async-done | bytes 3538976 | tf_op jit(solution)/shard_map/all_to_all | solution.py:31
  242.6 4.7 %all-to-all-start.1 = ((bf16[72,96,256]{2,0,1:T(8,128)(2,1)}), bf16[72,96,256]{2,0,1:T(8,128)(2,1)}, u32[]{:S(2)}, u32[]{:S(2)}) async-start(bf16[72,96,256]{2,0,1:T(8,128)(2,1)} %copy.61), calls=%async_computation.1 | async-start | bytes 7077888 | tf_op jit(solution)/shard_map/all_to_all | solution.py:31
  247.3 0.0 all-reduce.3.cloned.1.call-start
  247.4 2.5 copy.72
  249.9 2.3 copy.73
  252.2 2.4 copy.71
  254.6 71.7 %all-to-all-done.1 = bf16[72,96,256]{2,0,1:T(8,128)(2,1)} async-done(((bf16[72,96,256]{2,0,1:T(8,128)(2,1)}), bf16[72,96,256]{2,0,1:T(8,128)(2,1)}, u32[]{:S(2)}, u32[]{:S(2)}) %all-to-all-start.1) | async-done | bytes 3538976 | tf_op jit(solution)/shard_map/all_to_all | solution.py:31
  326.4 2.5 copy.63
  328.9 0.0 copy-start.4
  328.9 2.1 convolution_bitcast_fusion.1
  331.0 0.2 copy-done
  331.2 2.0 convolution_bitcast_fusion
  333.2 0.0 all-reduce.3.cloned.1.call-update
  333.2 3.4 convolution_convert_fusion.3
  336.6 2.3 copy.75
  338.9 3.4 convolution_convert_fusion.4
  342.3 1.3 copy.74
  343.6 57.5 %all-reduce.3.cloned.1.call-done = (f32[24,64,256]{2,1,0:T(8,128)}, f32[24,64,256]{2,1,0:T(8,128)}) async-done(((f32[24,64,256]{2,1,0:T(8,128)}, f32[24,64,256]{2,1,0:T(8,128)}), (f32[24,64,256]{2,1,0:T(8,128)}, f32[24,64,256]{2,1,0:T(8,128)})) %all-reduce.3.cloned.1.call-update) | async-done | bytes 3145744 | tf_op jit(solution)/shard_map/psum | solution.py:65
  401.1 2.7 copy.80
  403.8 2.7 copy.81
  (8 shorter events, 0.0 us)
Async XLA Ops:
  7.2 95.9 %all-gather.3.cloned.1.call-start = ((), (), s32[]{:S(2)}) async-start(), calls=%async_computation.3 | async-start | bytes 6488064 | tf_op jit(solution)/shard_map/all_gather | solution.py:24
  11.7 55.4 %all-to-all-start = ((bf16[4,2,72,1536]{3,2,1,0:T(8,128)(2,1)}), bf16[4,2,72,1536]{3,2,1,0:T(8,128)(2,1)}, u32[]{:S(2)}, u32[]{:S(2)}) async-start(bf16[4,2,72,1536]{3,2,1,0:T(8,128)(2,1)} %pad_maximum_fusion), calls=%async_computation | async-start | bytes 3538944 | tf_op jit(solution)/shard_map/all_to_all | solution.py:42
  108.1 1.4 copy-start.3
  116.0 2.4 copy-start.2
  159.1 83.5 %all-to-all-start.2 = ((bf16[72,96,256]{2,0,1:T(8,128)(2,1)}), bf16[72,96,256]{2,0,1:T(8,128)(2,1)S(1)}, u32[]{:S(2)}, u32[]{:S(2)}) async-start(bf16[72,96,256]{2,0,1:T(8,128)(2,1)} %copy.69), calls=%async_computation.2 | async-start | bytes 7077888 | tf_op jit(solution)/shard_map/all_to_all | solution.py:31
  242.6 9.6 %copy-start.1 = (bf16[72,96,256]{2,0,1:T(8,128)(2,1)}, bf16[72,96,256]{2,0,1:T(8,128)(2,1)S(1)}, u32[]{:S(2)}) copy-start(bf16[72,96,256]{2,0,1:T(8,128)(2,1)S(1)} %all-to-all-done.2) | copy-start | bytes 10616836
  242.6 83.8 %all-to-all-start.1 = ((bf16[72,96,256]{2,0,1:T(8,128)(2,1)}), bf16[72,96,256]{2,0,1:T(8,128)(2,1)}, u32[]{:S(2)}, u32[]{:S(2)}) async-start(bf16[72,96,256]{2,0,1:T(8,128)(2,1)} %copy.61), calls=%async_computation.1 | async-start | bytes 7077888 | tf_op jit(solution)/shard_map/all_to_all | solution.py:31
  247.3 153.8 %all-reduce.3.cloned.1.call-start = ((), (), s32[]{:S(2)}) async-start(), calls=%async_computation.4 | async-start | bytes 6291456 | tf_op jit(solution)/shard_map/psum | solution.py:65
  326.4 2.5 copy-start.5
  328.9 2.3 copy-start
  328.9 2.3 copy-start.4
Sparse Core Ops, SparseCore 0:
  11.4 91.5 all-gather.2
  333.3 67.7 all-reduce.2

commit v3 on v2

--- a/solution.py
+++ b/solution.py
@@ -43,8 +43,9 @@
     both = both.reshape(n_block, 2, mine, up_first.shape[0], width)
     both = both.transpose(1, 0, 3, 2, 4).reshape(2, blocks, mine, width)
     inputs, outgrads = both[0], both[1]
-    weights = gather_weights(jnp.stack([up_first, down_last]), n_dp, n_block)
-    first_w, last_w = weights[0], weights[1]
+    first_w = gather_weights(up_first[None], n_dp, n_block)[0]
+    later, first_w = lax.optimization_barrier((down_last, first_w))
+    last_w = gather_weights(later[None], n_dp, n_block)[0]
     first = jnp.einsum("rtk,rkc->rtc", inputs, first_w, preferred_element_type=flt).astype(half)
     grad_mixed = jnp.einsum("qtk,qkc->qtc", outgrads, last_w, preferred_element_type=flt).astype(half)
     pre = jnp.einsum("rtc,csr->tsc", first, up_mix, preferred_element_type=flt).astype(half)
@@ -62,6 +63,7 @@
     grad_first = to_blocks(grad_first_tok)
     encoded = jnp.einsum("tqc,qkc->tqk", mixed, down_last, preferred_element_type=flt).astype(half)
     grad_firstw = jnp.einsum("trk,trc->rkc", own_in, grad_first, preferred_element_type=flt)
+    grad_firstw, summed_last = lax.optimization_barrier((grad_firstw, summed_last))
     summed_first = lax.psum(grad_firstw, "dp")
     grad_in = jnp.einsum("trc,rkc->trk", grad_first, up_first, preferred_element_type=flt).astype(half)
     return (

time: 415 us -> 408 us (0.983)
  waiting for transfers between devices: 245 us -> 233 us
  matrix products: 50.1 us -> 56.6 us
    all_gather x1 -> x2, waiting for transfers between devices: 21.6 us -> 72.9 us  [gather_weights(): full = lax.all_gather(mine, ('block', 'dp'))]
    all_to_all x1, waiting for transfers between devices: 32.1 us -> 0.01 us  [shards(): both = lax.all_to_all(both, 'block', 0, 0, tiled=True)]
    all_to_all x2, waiting for transfers between devices: 134 us -> 112 us  [to_blocks(): lax.all_to_all(panel, 'block', split_axis=1, concat_axis=0, tiled=True)]
    psum x1, waiting for transfers between devices: 57.5 us -> 47.8 us  [shards(): summed_first = lax.psum(grad_firstw, 'dp')]
    slice x3 -> x0, local copies, waits for them, and re-layouts: 7.96 us -> none  [shards(): first_w, last_w = (weights[0], weights[1])]
    transpose x0 -> x2, local copies, waits for them, and re-layouts: none -> 6.42 us  [gather_weights(): full = full.transpose(2, 0, 3, 1, 4, 5)]
    unnamed x20 -> x22, local copies, waits for them, and re-layouts: 32.2 us -> 28.4 us
  transfers between devices with their start and end apart: 5 -> 7, of which waited for: 5 -> 4; matrix products, arithmetic and copies ran while one was open for 17% -> 33% of each run, Pallas kernels for 0% -> 0%
where the time goes in v3:
time: 408 us; the launch traced here: 407 us
  waiting for transfers between devices  233 us (57%)
  local copies, waits for them, and re-layouts  84.3 us (21%)
  matrix products  56.6 us (14%)
  starting transfers between devices  16.3 us (4%)
  between operations  13.9 us (3%)
    all_to_all x2, waiting for transfers between devices, to_blocks(): lax.all_to_all(panel, 'block', split_axis=1, concat_axis=0, tiled=True)  112 us
    all_gather x2, waiting for transfers between devices, gather_weights(): full = lax.all_gather(mine, ('block', 'dp'))  72.9 us
    psum x1, waiting for transfers between devices, shards(): summed_first = lax.psum(grad_firstw, 'dp')  47.8 us
    unnamed x22, local copies, waits for them, and re-layouts  28.4 us
    dot_general x1, matrix products, shards(): jnp.einsum('tsc,csr->trc', grad_pre, up_mix, preferred_element_type=flt)  16.1 us
    dot_general x1, matrix products, shards(): jnp.einsum('rtc,csr->tsc', first, up_mix, preferred_element_type=flt)  11 us
    dot_general x1, matrix products, shards(): jnp.einsum('tsc,cqs->tqc', hidden, down_mix, preferred_element_type=flt)  10.1 us
    slice x3, local copies, waits for them, and re-layouts, shards(): inputs, outgrads = (both[0], both[1])  10.1 us
  transfers between devices with their start and end apart: 7, of which 4 were waited for; matrix products, arithmetic and copies ran while one was open for 33% of the time, Pallas kernels for 0%

profile of v3, /device:TPU:0, one launch (start us, length us, event | category | flops | bytes accessed | tf_op | source)
XLA Modules:
  0.0 406.9 jit_solution(8421656263933353058)
XLA Ops:
  7.2 0.0 all-gather.5.cloned.1.call-start
  7.2 1.6 constant_dynamic-slice_fusion.1
  8.8 0.0 all-gather.5.cloned.1.call-update
  8.9 2.8 pad_maximum_fusion
  11.7 6.3 %all-to-all-start = ((bf16[4,2,72,1536]{3,2,1,0:T(8,128)(2,1)}), bf16[4,2,72,1536]{3,2,1,0:T(8,128)(2,1)S(1)}, u32[]{:S(2)}, u32[]{:S(2)}) async-start(bf16[4,2,72,1536]{3,2,1,0:T(8,128)(2,1)} %pad_maximum_fusion), calls=%async_computation | async-start | bytes 3538944 | tf_op jit(solution)/shard_map/all_to_all | solution.py:42
  18.0 72.9 %all-gather.5.cloned.1.call-done = bf16[768,8,256]{2,1,0:T(8,128)(2,1)} async-done(((bf16[24,8,256]{2,1,0:T(8,128)(2,1)}), bf16[768,8,256]{2,1,0:T(8,128)(2,1)}) %all-gather.5.cloned.1.call-update) | async-done | bytes 3145744 | tf_op jit(solution)/shard_map/all_gather | solution.py:24
  90.9 4.0 copy.57
  94.9 0.7 constant_dynamic-slice_fusion
  95.5 0.0 all-gather.7.cloned.1.call-update
  95.6 8.5 %copy.59 = bf16[256,96,96]{2,1,0:T(8,128)(2,1)} copy(bf16[256,96,96]{0,2,1:T(8,128)(2,1)} %param.8) | data formatting | bytes 9437184 | tf_op args[2]
  104.0 8.4 %copy.60 = bf16[256,96,96]{2,1,0:T(8,128)(2,1)} copy(bf16[256,96,96]{0,2,1:T(8,128)(2,1)} %param.9) | data formatting | bytes 9437184 | tf_op args[3]
  112.4 3.5 reshape.38
  115.9 3.8 fusion.34
  119.7 3.8 copy.56
  123.6 5.3 %convolution_convert_fusion.2 = bf16[96,72,256]{2,1,0:T(8,128)(2,1)} fusion(bf16[96,72,64]{1,2,0:T(8,128)(2,1)} %bitcast.98, bf16[96,64,256]{2,1,0:T(8,128)(2,1)} %bitcast.95), kind=kOutput, calls=%fused_computation.25 | convolution fusion | flops 228261888 | bytes 7569408 | tf_op jit(solution)/shard_map/rtk,rkc->rtc/dot_general | solution.py:49
  128.9 7.2 %copy.58 = bf16[96,72,256]{0,1,2:T(8,128)(2,1)} copy(bf16[96,72,256]{2,1,0:T(8,128)(2,1)} %convolution_convert_fusion.2) | data formatting | bytes 7077888 | tf_op jit(solution)/shard_map/convert_element_type | solution.py:49
  136.0 11.0 %convolution_convert_fusion = bf16[256,72,96]{2,1,0:T(8,128)(2,1)} fusion(bf16[96,72,256]{0,1,2:T(8,128)(2,1)} %copy.58, bf16[256,96,96]{2,1,0:T(8,128)(2,1)} %copy.59), kind=kOutput, calls=%fused_computation.23 | convolution fusion | flops 341508096 | bytes 11796480 | tf_op jit(solution)/shard_map/rtc,csr->tsc/dot_general | solution.py:51
  147.0 10.1 %convert_bitcast_fusion.1 = bf16[72,96,256]{1,0,2:T(8,128)(2,1)} fusion(bf16[256,96,96]{2,1,0:T(8,128)(2,1)} %copy.60, bf16[256,72,96]{2,1,0:T(8,128)(2,1)} %convolution_convert_fusion), kind=kOutput, calls=%fused_computation.16 | convolution fusion | flops 359202816 | bytes 11796480 | tf_op jit(solution)/shard_map/tsc,cqs->tqc/dot_general | solution.py:54
  157.2 7.3 %copy.61 = bf16[72,96,256]{2,0,1:T(8,128)(2,1)} copy(bf16[72,96,256]{1,0,2:T(8,128)(2,1)} %convert_bitcast_fusion.1) | data formatting | bytes 7077888 | tf_op jit(solution)/shard_map/convert_element_type | solution.py:54
  164.5 4.9 %all-to-all-start.1 = ((bf16[72,96,256]{2,0,1:T(8,128)(2,1)}), bf16[72,96,256]{2,0,1:T(8,128)(2,1)}, u32[]{:S(2)}, u32[]{:S(2)}) async-start(bf16[72,96,256]{2,0,1:T(8,128)(2,1)} %copy.61), calls=%async_computation.1 | async-start | bytes 7077888 | tf_op jit(solution)/shard_map/all_to_all | solution.py:31
  169.4 2.4 copy.64
  171.8 2.4 copy.65
  174.3 3.0 convolution_convert_fusion.1
  177.3 7.1 %copy.66 = bf16[96,72,256]{0,1,2:T(8,128)(2,1)} copy(bf16[96,72,256]{2,1,0:T(8,128)(2,1)} %convolution_convert_fusion.1) | data formatting | bytes 7077888 | tf_op jit(solution)/shard_map/convert_element_type | solution.py:50
  184.5 16.1 %convert_bitcast_fusion = bf16[72,96,256]{1,0,2:T(8,128)(2,1)} fusion(bf16[256,96,96]{2,1,0:T(8,128)(2,1)} %copy.59, bf16[256,72,96]{2,1,0:T(8,128)(2,1)} %convolution_convert_fusion, bf16[96,72,256]{0,1,2:T(8,128)(2,1)} %copy.66, bf16[256,96,96]{2,1,0:T(8,128)(2,1)} %copy.60), kind=kOutput, calls=%fused_computation.15 | convolution fusion | flops 720175104 | bytes 20054016 | tf_op jit(solution)/shard_map/tsc,csr->trc/dot_general | solution.py:58
  200.6 7.3 %copy.69 = bf16[72,96,256]{2,0,1:T(8,128)(2,1)} copy(bf16[72,96,256]{1,0,2:T(8,128)(2,1)} %convert_bitcast_fusion) | data formatting | bytes 7077888 | tf_op jit(solution)/shard_map/convert_element_type | solution.py:58
  207.9 41.3 %all-to-all-done.1 = bf16[72,96,256]{2,0,1:T(8,128)(2,1)} async-done(((bf16[72,96,256]{2,0,1:T(8,128)(2,1)}), bf16[72,96,256]{2,0,1:T(8,128)(2,1)}, u32[]{:S(2)}, u32[]{:S(2)}) %all-to-all-start.1) | async-done | bytes 3538976 | tf_op jit(solution)/shard_map/all_to_all | solution.py:31
  249.2 4.7 %all-to-all-start.2 = ((bf16[72,96,256]{2,0,1:T(8,128)(2,1)}), bf16[72,96,256]{2,0,1:T(8,128)(2,1)}, u32[]{:S(2)}, u32[]{:S(2)}) async-start(bf16[72,96,256]{2,0,1:T(8,128)(2,1)} %copy.69), calls=%async_computation.2 | async-start | bytes 7077888 | tf_op jit(solution)/shard_map/all_to_all | solution.py:31
  253.9 0.0 all-reduce.3.cloned.1.call-start
  254.0 0.7 copy.73
  254.7 2.4 copy.63
  257.1 1.8 copy-done.1
  258.9 2.1 convolution_bitcast_fusion
  261.0 0.0 all-reduce.3.cloned.1.call-update
  261.0 0.3 all-reduce.5.cloned.1.call-start
  261.3 0.7 copy.72
  262.0 71.0 %all-to-all-done.2 = bf16[72,96,256]{2,0,1:T(8,128)(2,1)} async-done(((bf16[72,96,256]{2,0,1:T(8,128)(2,1)}), bf16[72,96,256]{2,0,1:T(8,128)(2,1)}, u32[]{:S(2)}, u32[]{:S(2)}) %all-to-all-start.2) | async-done | bytes 3538976 | tf_op jit(solution)/shard_map/all_to_all | solution.py:31
  333.0 2.4 copy.71
  335.5 1.8 copy-done.2
  337.2 2.1 convolution_bitcast_fusion.1
  339.3 0.0 all-reduce.5.cloned.1.call-update
  339.4 3.2 convolution_convert_fusion.4
  342.6 1.3 copy.74
  343.9 3.5 convolution_convert_fusion.3
  347.4 1.3 copy.75
  348.8 47.8 %all-reduce.5.cloned.1.call-done = f32[24,64,256]{2,1,0:T(8,128)} async-done(((f32[24,64,256]{2,1,0:T(8,128)}), f32[24,64,256]{2,1,0:T(8,128)}) %all-reduce.5.cloned.1.call-update) | async-done | bytes 1572880 | tf_op jit(solution)/shard_map/psum | solution.py:67
  396.6 2.7 copy.80
  399.3 1.1 copy.81
  (16 shorter events, 0.0 us)
Async XLA Ops:
  7.2 87.7 %copy-start = (bf16[24,64,256]{2,1,0:T(8,128)(2,1)S(1)}, bf16[24,64,256]{2,1,0:T(8,128)(2,1)}, u32[]{:S(2)}) copy-start(bf16[24,64,256]{2,1,0:T(8,128)(2,1)} %param.10) | copy-start | bytes 2359300
  7.2 83.7 %all-gather.5.cloned.1.call-start = ((), (), s32[]{:S(2)}) async-start(), calls=%async_computation.5 | async-start | bytes 3244032 | tf_op jit(solution)/shard_map/all_gather | solution.py:24
  11.7 100.7 %all-to-all-start = ((bf16[4,2,72,1536]{3,2,1,0:T(8,128)(2,1)}), bf16[4,2,72,1536]{3,2,1,0:T(8,128)(2,1)S(1)}, u32[]{:S(2)}, u32[]{:S(2)}) async-start(bf16[4,2,72,1536]{3,2,1,0:T(8,128)(2,1)} %pad_maximum_fusion), calls=%async_computation | async-start | bytes 3538944 | tf_op jit(solution)/shard_map/all_to_all | solution.py:42
  18.0 153.8 %all-gather.7.cloned.1.call-start = ((), (), s32[]{:S(2)}) async-start(), calls=%async_computation.6 | async-start | bytes 3244032 | tf_op jit(solution)/shard_map/all_gather | solution.py:24
  164.5 84.7 %all-to-all-start.1 = ((bf16[72,96,256]{2,0,1:T(8,128)(2,1)}), bf16[72,96,256]{2,0,1:T(8,128)(2,1)}, u32[]{:S(2)}, u32[]{:S(2)}) async-start(bf16[72,96,256]{2,0,1:T(8,128)(2,1)} %copy.61), calls=%async_computation.1 | async-start | bytes 7077888 | tf_op jit(solution)/shard_map/all_to_all | solution.py:31
  171.8 2.4 copy-start.3
  207.9 46.0 %copy-start.4 = (bf16[288,1536]{1,0:T(8,128)(2,1)S(1)}, bf16[288,1536]{1,0:T(8,128)(2,1)}, u32[]{:S(2)}) copy-start(bf16[288,1536]{1,0:T(8,128)(2,1)} %param.11) | copy-start | bytes 2654212
  249.2 83.9 %all-to-all-start.2 = ((bf16[72,96,256]{2,0,1:T(8,128)(2,1)}), bf16[72,96,256]{2,0,1:T(8,128)(2,1)}, u32[]{:S(2)}, u32[]{:S(2)}) async-start(bf16[72,96,256]{2,0,1:T(8,128)(2,1)} %copy.69), calls=%async_computation.2 | async-start | bytes 7077888 | tf_op jit(solution)/shard_map/all_to_all | solution.py:31
  253.9 85.4 %all-reduce.3.cloned.1.call-start = ((), (), s32[]{:S(2)}) async-start(), calls=%async_computation.3 | async-start | bytes 3145728 | tf_op jit(solution)/shard_map/psum | solution.py:62
  257.1 1.8 copy-start.1
  257.1 4.2 %copy-start.5 = (bf16[288,1536]{1,0:T(8,128)(2,1)S(1)}, bf16[288,1536]{1,0:T(8,128)(2,1)}, u32[]{:S(2)}) copy-start(bf16[288,1536]{1,0:T(8,128)(2,1)} %param.6) | copy-start | bytes 2654212
  261.0 135.5 %all-reduce.5.cloned.1.call-start = ((), (), s32[]{:S(2)}) async-start(), calls=%async_computation.4 | async-start | bytes 3145728 | tf_op jit(solution)/shard_map/psum | solution.py:67
  335.5 1.8 copy-start.2
  343.9 55.4 %copy-start.6 = (f32[24,64,256]{2,1,0:T(8,128)S(1)}, f32[24,64,256]{2,1,0:T(8,128)}, u32[]{:S(2)}) copy-start(f32[24,64,256]{2,1,0:T(8,128)} %all-reduce.3.cloned.1.call-done) | copy-start | bytes 4718596
Sparse Core Ops, SparseCore 0:
  11.5 79.3 all-gather.4
  95.7 57.7 all-gather.6
  261.2 59.3 all-reduce.2
  339.5 57.0 all-reduce.4
